TPU v7x, 32 devices: a whole 2x2x4 slice. The times are simulated.
32 devices in a mesh: dp: 4 (over y, core), fsdp: 8 (over z, x).
Axes of the slice: x: 2, y: 2, z: 4, core: 2. Of those that a mesh axis runs over, the one named last changes fastest.
Arguments:
- hidden_in: bfloat16 [16384, 768], P(('dp', 'fsdp')), may hold values from -6 to 6
- output_grad: bfloat16 [16384, 768], P(('dp', 'fsdp')), may hold values from -6 to 6
- encoder_states: bfloat16 [64, 512, 768], P(('dp', 'fsdp')), may hold values from -6 to 6
- language_ids: int32 [64], P(('dp', 'fsdp')), may hold values from 0 to 7
- source_index: int32 [64], P(('dp', 'fsdp')), may hold values from 0 to 1
- bucket_ids: int32 [256, 256], replicated, may hold values from 0 to 31, as said below
- language_table: bfloat16 [8, 768], P(None, ('dp', 'fsdp')), may hold values from -3 to 3
- bucket_table: bfloat16 [32, 12], replicated, may hold values from -4 to 4
- self_gain: bfloat16 [768], P(('dp', 'fsdp')), may hold values from 0.5 to 1.5
- self_query: bfloat16 [768, 768], P(('dp', 'fsdp')), may hold values from -0.02734375 to 0.02734375
- self_key: bfloat16 [768, 768], P(('dp', 'fsdp')), may hold values from -0.21875 to 0.21875
- self_value: bfloat16 [768, 768], P(('dp', 'fsdp')), may hold values from -0.21875 to 0.21875
- self_out: bfloat16 [768, 768], P(('dp', 'fsdp')), may hold values from -1.25 to 1.25
- cross_gain: bfloat16 [768], P(('dp', 'fsdp')), may hold values from 0.5 to 1.5
- cross_query: bfloat16 [768, 768], P(('dp', 'fsdp')), may hold values from -0.02734375 to 0.02734375
- cross_key: bfloat16 [768, 768], P(('dp', 'fsdp')), may hold values from -0.21875 to 0.21875
- cross_value: bfloat16 [768, 768], P(('dp', 'fsdp')), may hold values from -0.21875 to 0.21875
- cross_out: bfloat16 [768, 768], P(('dp', 'fsdp')), may hold values from -1.75 to 1.75
- feed_gain: bfloat16 [768], P(('dp', 'fsdp')), may hold values from 0.5 to 1.5
- inner_weight: bfloat16 [768, 3072], P(('dp', 'fsdp')), may hold values from -0.21875 to 0.21875
- outer_weight: bfloat16 [3072, 768], P(('dp', 'fsdp')), may hold values from -0.109375 to 0.109375
Outputs:
- hidden_out: bfloat16 [16384, 768], P(('dp', 'fsdp'))
- hidden_in_grad: float32 [16384, 768], P(('dp', 'fsdp'))
- encoder_grad: float32 [64, 512, 768], P(('dp', 'fsdp'))
- language_table_grad: float32 [8, 768], P(None, ('dp', 'fsdp'))
- bucket_table_grad: float32 [32, 12], replicated
- self_gain_grad: float32 [768], P(('dp', 'fsdp'))
- self_query_grad: float32 [768, 768], P(('dp', 'fsdp'))
- self_key_grad: float32 [768, 768], P(('dp', 'fsdp'))
- self_value_grad: float32 [768, 768], P(('dp', 'fsdp'))
- self_out_grad: float32 [768, 768], P(('dp', 'fsdp'))
- cross_gain_grad: float32 [768], P(('dp', 'fsdp'))
- cross_query_grad: float32 [768, 768], P(('dp', 'fsdp'))
- cross_key_grad: float32 [768, 768], P(('dp', 'fsdp'))
- cross_value_grad: float32 [768, 768], P(('dp', 'fsdp'))
- cross_out_grad: float32 [768, 768], P(('dp', 'fsdp'))
- feed_gain_grad: float32 [768], P(('dp', 'fsdp'))
- inner_weight_grad: float32 [768, 3072], P(('dp', 'fsdp'))
- outer_weight_grad: float32 [3072, 768], P(('dp', 'fsdp'))
Inputs may be any that keep to these rules, and one draw needn't show every extreme that they name: bucket_ids[i, j] is the bucket of the distance between the positions of query i and key j, the positions rising by 1 or 2 from token to token; exact buckets below 16, logarithmic ones up to a distance of 128 and above; 0 where j > i.
All inputs are finite; a program needn't handle non-finite values.
Results may differ from a plain program's by a relative error of at most 0.019.
Values may be sent and summed in bfloat16 or wider, within the bound.
A program may use at most 192 MiB of HBM per device.

v0:
```python
import jax
import jax.numpy as jnp
from jax import lax
from jax.sharding import PartitionSpec as P

H = 12
HEAD = 64
SEQ_BLOCK = 2


EPSILON = 1e-06
PRECISE = lax.Precision.HIGHEST
NEGATIVE = -1e30


def to_low(value):
    return value.astype(jnp.bfloat16)


def norm_scale(hidden, gain):
    return hidden * lax.rsqrt(jnp.mean(hidden * hidden, axis=-1, keepdims=True) + EPSILON) * gain


def matmul(left, right):
    return jnp.dot(left, right, preferred_element_type=jnp.float32)


def left_product(left, right):
    return lax.dot_general(
        left, right, (((0,), (0,)), ((), ())), preferred_element_type=jnp.float32
    )


def right_product(left, right):
    return lax.dot_general(
        left, right, (((1,), (1,)), ((), ())), preferred_element_type=jnp.float32
    )


def split_heads(array):
    return array.reshape(array.shape[:-1] + (H, HEAD))


def score_block(queries, key_rows, offset):
    scores = jnp.einsum(
        "sqhe,skhe->shqk",
        split_heads(queries),
        split_heads(key_rows),
        preferred_element_type=jnp.float32,
    )
    return scores + offset


def attend_forward(queries, key_rows, value_rows, offset):
    scores = score_block(queries, key_rows, offset)
    top_score = jnp.max(scores, axis=-1, keepdims=True)
    log_total = top_score + jnp.log(jnp.sum(jnp.exp(scores - top_score), axis=-1, keepdims=True))
    weights = to_low(jnp.exp(scores - log_total))
    context = jnp.einsum(
        "shqk,skhe->sqhe", weights, split_heads(value_rows), preferred_element_type=jnp.float32
    )
    return (to_low(context).reshape(queries.shape), log_total)


def attend_backward(queries, key_rows, value_rows, offset, log_total, context_grad, with_bias):
    scores = score_block(queries, key_rows, offset)
    probs = jnp.exp(scores - log_total)
    weights = to_low(probs)
    grad_heads = split_heads(context_grad)
    value_grad = jnp.einsum(
        "shqk,sqhe->skhe", weights, grad_heads, preferred_element_type=jnp.float32
    )
    prob_grad = jnp.einsum(
        "sqhe,skhe->shqk", grad_heads, split_heads(value_rows), preferred_element_type=jnp.float32
    )
    score_grad = to_low(probs * (prob_grad - jnp.sum(probs * prob_grad, axis=-1, keepdims=True)))
    query_grad = jnp.einsum(
        "shqk,skhe->sqhe", score_grad, split_heads(key_rows), preferred_element_type=jnp.float32
    )
    key_grad = jnp.einsum(
        "shqk,sqhe->skhe", score_grad, split_heads(queries), preferred_element_type=jnp.float32
    )
    grads = (
        query_grad.reshape(queries.shape),
        key_grad.reshape(key_rows.shape),
        value_grad.reshape(value_rows.shape),
    )
    if with_bias:
        return grads + (jnp.sum(score_grad.astype(jnp.float32), axis=0),)
    return grads


def local(
    hidden_in,
    output_grad,
    encoder_states,
    language_ids,
    source_index,
    bucket_ids,
    language_table,
    bucket_table,
    self_gain,
    self_query,
    self_key,
    self_value,
    self_out,
    cross_gain,
    cross_query,
    cross_key,
    cross_value,
    cross_out,
    feed_gain,
    inner_weight,
    outer_weight,
):
    seq_count = language_ids.shape[0]
    length = bucket_ids.shape[0]
    tokens = seq_count * length
    enc_count = encoder_states.shape[0]
    enc_length = encoder_states.shape[1]
    width = hidden_in.shape[1]
    blocks = seq_count // SEQ_BLOCK

    def to_blocks(array, rows):
        return array.reshape(blocks, SEQ_BLOCK, rows, array.shape[-1])

    gain_one, table_whole, query_whole, key_whole, value_whole, out_whole = (
        lax.all_gather(self_gain, ("dp", "fsdp"), axis=0, tiled=True),
        lax.all_gather(language_table, ("dp", "fsdp"), axis=1, tiled=True),
        lax.all_gather(self_query, ("dp", "fsdp"), axis=0, tiled=True),
        lax.all_gather(self_key, ("dp", "fsdp"), axis=0, tiled=True),
        lax.all_gather(self_value, ("dp", "fsdp"), axis=0, tiled=True),
        lax.all_gather(self_out, ("dp", "fsdp"), axis=0, tiled=True),
    )
    language_hot = (language_ids[:, None] == jnp.arange(table_whole.shape[0])[None, :]).astype(
        jnp.float32
    )
    language_rows = jnp.dot(language_hot, table_whole.astype(jnp.float32), precision=PRECISE)
    start_state = (
        hidden_in.astype(jnp.float32).reshape(seq_count, length, width) + language_rows[:, None, :]
    ).reshape(tokens, width)
    first_norm = to_low(norm_scale(start_state, gain_one.astype(jnp.float32)))
    self_queries = to_low(matmul(first_norm, query_whole))
    self_keys = to_low(matmul(first_norm, key_whole))
    self_values = to_low(matmul(first_norm, value_whole))
    bucket_hot = (
        bucket_ids[:, :, None] == jnp.arange(bucket_table.shape[0])[None, None, :]
    ).astype(jnp.float32)
    position_bias = jnp.einsum(
        "ijb,bh->hij", bucket_hot, bucket_table.astype(jnp.float32), precision=PRECISE
    )
    positions = jnp.arange(length)
    masked_bias = jnp.where(
        (positions[:, None] >= positions[None, :])[None], position_bias, NEGATIVE
    )

    def self_forward(block_items):
        return attend_forward(block_items[0], block_items[1], block_items[2], masked_bias)

    self_context, self_total = lax.map(
        self_forward,
        (
            to_blocks(self_queries, length),
            to_blocks(self_keys, length),
            to_blocks(self_values, length),
        ),
    )
    self_context = self_context.reshape(tokens, -1)
    mid_state = start_state + matmul(self_context, out_whole)
    gain_two, cquery_whole, ckey_whole, cvalue_whole, cout_whole = (
        lax.all_gather(cross_gain, ("dp", "fsdp"), axis=0, tiled=True),
        lax.all_gather(cross_query, ("dp", "fsdp"), axis=0, tiled=True),
        lax.all_gather(cross_key, ("dp", "fsdp"), axis=0, tiled=True),
        lax.all_gather(cross_value, ("dp", "fsdp"), axis=0, tiled=True),
        lax.all_gather(cross_out, ("dp", "fsdp"), axis=0, tiled=True),
    )
    second_norm = to_low(norm_scale(mid_state, gain_two.astype(jnp.float32)))
    cross_queries = to_low(matmul(second_norm, cquery_whole))
    encoder_flat = encoder_states.reshape(enc_count * enc_length, width)
    source_keys = to_low(matmul(encoder_flat, ckey_whole)).reshape(enc_count, enc_length, -1)
    source_values = to_low(matmul(encoder_flat, cvalue_whole)).reshape(enc_count, enc_length, -1)
    source_hot = (source_index[:, None] == jnp.arange(enc_count)[None, :]).astype(jnp.float32)
    source_low = to_low(source_hot)
    picked_keys = to_low(
        jnp.einsum("se,emc->smc", source_low, source_keys, preferred_element_type=jnp.float32)
    )
    picked_values = to_low(
        jnp.einsum("se,emc->smc", source_low, source_values, preferred_element_type=jnp.float32)
    )

    def cross_forward(block_items):
        return attend_forward(block_items[0], block_items[1], block_items[2], 0.0)

    cross_context, cross_total = lax.map(
        cross_forward,
        (
            to_blocks(cross_queries, length),
            picked_keys.reshape(blocks, SEQ_BLOCK, enc_length, -1),
            picked_values.reshape(blocks, SEQ_BLOCK, enc_length, -1),
        ),
    )
    cross_context = cross_context.reshape(tokens, -1)
    late_state = mid_state + matmul(cross_context, cout_whole)
    gain_three, inner_whole, outer_whole = (
        lax.all_gather(feed_gain, ("dp", "fsdp"), axis=0, tiled=True),
        lax.all_gather(inner_weight, ("dp", "fsdp"), axis=0, tiled=True),
        lax.all_gather(outer_weight, ("dp", "fsdp"), axis=0, tiled=True),
    )
    third_norm = to_low(norm_scale(late_state, gain_three.astype(jnp.float32)))
    expanded = matmul(third_norm, inner_whole)
    activated = to_low(jax.nn.gelu(expanded, approximate=True))
    hidden_out = (late_state + matmul(activated, outer_whole)).astype(jnp.bfloat16)
    gain_three, inner_whole, outer_whole = (
        lax.all_gather(feed_gain, ("dp", "fsdp"), axis=0, tiled=True),
        lax.all_gather(inner_weight, ("dp", "fsdp"), axis=0, tiled=True),
        lax.all_gather(outer_weight, ("dp", "fsdp"), axis=0, tiled=True),
    )
    top_grad = output_grad.astype(jnp.float32)
    outer_full = left_product(activated, output_grad)
    activated_grad = right_product(output_grad, outer_whole)
    gelu_value, gelu_back = jax.vjp(jax.nn.gelu, expanded)
    expanded_grad = to_low(gelu_back(activated_grad)[0])
    inner_full = left_product(third_norm, expanded_grad)
    third_grad = right_product(expanded_grad, inner_whole)
    norm_value, norm_back = jax.vjp(norm_scale, late_state, gain_three.astype(jnp.float32))
    state_back, feed_gain_full = norm_back(third_grad)
    late_grad = top_grad + state_back
    feed_gain_part, inner_part, outer_part = (
        lax.psum_scatter(feed_gain_full, ("dp", "fsdp"), scatter_dimension=0, tiled=True),
        lax.psum_scatter(inner_full, ("dp", "fsdp"), scatter_dimension=0, tiled=True),
        lax.psum_scatter(outer_full, ("dp", "fsdp"), scatter_dimension=0, tiled=True),
    )
    gain_two, cquery_whole, ckey_whole, cvalue_whole, cout_whole = (
        lax.all_gather(cross_gain, ("dp", "fsdp"), axis=0, tiled=True),
        lax.all_gather(cross_query, ("dp", "fsdp"), axis=0, tiled=True),
        lax.all_gather(cross_key, ("dp", "fsdp"), axis=0, tiled=True),
        lax.all_gather(cross_value, ("dp", "fsdp"), axis=0, tiled=True),
        lax.all_gather(cross_out, ("dp", "fsdp"), axis=0, tiled=True),
    )
    cross_low = to_low(late_grad)
    cout_full = left_product(cross_context, cross_low)
    cross_context_grad = to_low(right_product(cross_low, cout_whole))

    def cross_backward(block_items):
        return attend_backward(
            block_items[0],
            block_items[1],
            block_items[2],
            0.0,
            block_items[3],
            block_items[4],
            False,
        )

    cquery_part, ckey_part, cvalue_part = lax.map(
        cross_backward,
        (
            to_blocks(cross_queries, length),
            picked_keys.reshape(blocks, SEQ_BLOCK, enc_length, -1),
            picked_values.reshape(blocks, SEQ_BLOCK, enc_length, -1),
            cross_total,
            to_blocks(cross_context_grad, length),
        ),
    )
    cquery_low = to_low(cquery_part.reshape(tokens, -1))
    source_key_grad = to_low(
        jnp.einsum(
            "se,smc->emc",
            source_hot,
            ckey_part.reshape(seq_count, enc_length, -1),
            precision=PRECISE,
        ).reshape(enc_count * enc_length, -1)
    )
    source_value_grad = to_low(
        jnp.einsum(
            "se,smc->emc",
            source_hot,
            cvalue_part.reshape(seq_count, enc_length, -1),
            precision=PRECISE,
        ).reshape(enc_count * enc_length, -1)
    )
    cquery_full = left_product(second_norm, cquery_low)
    ckey_full = left_product(encoder_flat, source_key_grad)
    cvalue_full = left_product(encoder_flat, source_value_grad)
    encoder_grad = (
        right_product(source_key_grad, ckey_whole) + right_product(source_value_grad, cvalue_whole)
    ).reshape(enc_count, enc_length, width)
    second_grad = right_product(cquery_low, cquery_whole)
    norm_value, norm_back = jax.vjp(norm_scale, mid_state, gain_two.astype(jnp.float32))
    state_back, cross_gain_full = norm_back(second_grad)
    mid_grad = late_grad + state_back
    cgain_part, cquery_part_sum, ckey_part_sum, cvalue_part_sum, cout_part = (
        lax.psum_scatter(cross_gain_full, ("dp", "fsdp"), scatter_dimension=0, tiled=True),
        lax.psum_scatter(cquery_full, ("dp", "fsdp"), scatter_dimension=0, tiled=True),
        lax.psum_scatter(ckey_full, ("dp", "fsdp"), scatter_dimension=0, tiled=True),
        lax.psum_scatter(cvalue_full, ("dp", "fsdp"), scatter_dimension=0, tiled=True),
        lax.psum_scatter(cout_full, ("dp", "fsdp"), scatter_dimension=0, tiled=True),
    )
    gain_one, query_whole, key_whole, value_whole, out_whole = (
        lax.all_gather(self_gain, ("dp", "fsdp"), axis=0, tiled=True),
        lax.all_gather(self_query, ("dp", "fsdp"), axis=0, tiled=True),
        lax.all_gather(self_key, ("dp", "fsdp"), axis=0, tiled=True),
        lax.all_gather(self_value, ("dp", "fsdp"), axis=0, tiled=True),
        lax.all_gather(self_out, ("dp", "fsdp"), axis=0, tiled=True),
    )
    self_low = to_low(mid_grad)
    out_full = left_product(self_context, self_low)
    self_context_grad = to_low(right_product(self_low, out_whole))

    def self_backward(block_items):
        return attend_backward(
            block_items[0],
            block_items[1],
            block_items[2],
            masked_bias,
            block_items[3],
            block_items[4],
            True,
        )

    query_part, key_part, value_part, bias_part = lax.map(
        self_backward,
        (
            to_blocks(self_queries, length),
            to_blocks(self_keys, length),
            to_blocks(self_values, length),
            self_total,
            to_blocks(self_context_grad, length),
        ),
    )
    query_low = to_low(query_part.reshape(tokens, -1))
    key_low = to_low(key_part.reshape(tokens, -1))
    value_low = to_low(value_part.reshape(tokens, -1))
    table_full = jnp.einsum(
        "hij,ijb->bh", jnp.sum(bias_part, axis=0), bucket_hot, precision=PRECISE
    )
    bucket_table_grad = lax.psum(table_full, ("dp", "fsdp"))
    query_full = left_product(first_norm, query_low)
    key_full = left_product(first_norm, key_low)
    value_full = left_product(first_norm, value_low)
    first_grad = (
        right_product(query_low, query_whole)
        + right_product(key_low, key_whole)
        + right_product(value_low, value_whole)
    )
    norm_value, norm_back = jax.vjp(norm_scale, start_state, gain_one.astype(jnp.float32))
    state_back, self_gain_full = norm_back(first_grad)
    hidden_in_grad = mid_grad + state_back
    sequence_sums = jnp.sum(hidden_in_grad.reshape(seq_count, length, width), axis=1)
    language_full = left_product(language_hot, sequence_sums)
    sgain_part, language_part, query_sum, key_sum, value_sum, out_part = (
        lax.psum_scatter(self_gain_full, ("dp", "fsdp"), scatter_dimension=0, tiled=True),
        lax.psum_scatter(language_full, ("dp", "fsdp"), scatter_dimension=1, tiled=True),
        lax.psum_scatter(query_full, ("dp", "fsdp"), scatter_dimension=0, tiled=True),
        lax.psum_scatter(key_full, ("dp", "fsdp"), scatter_dimension=0, tiled=True),
        lax.psum_scatter(value_full, ("dp", "fsdp"), scatter_dimension=0, tiled=True),
        lax.psum_scatter(out_full, ("dp", "fsdp"), scatter_dimension=0, tiled=True),
    )
    return (
        hidden_out,
        hidden_in_grad,
        encoder_grad,
        language_part,
        bucket_table_grad,
        sgain_part,
        query_sum,
        key_sum,
        value_sum,
        out_part,
        cgain_part,
        cquery_part_sum,
        ckey_part_sum,
        cvalue_part_sum,
        cout_part,
        feed_gain_part,
        inner_part,
        outer_part,
    )


def solution(mesh):
    in_specs = (
        P(("dp", "fsdp"), None),
        P(("dp", "fsdp"), None),
        P(("dp", "fsdp"), None, None),
        P(("dp", "fsdp")),
        P(("dp", "fsdp")),
        P(),
        P(None, ("dp", "fsdp")),
        P(),
        P(("dp", "fsdp")),
        P(("dp", "fsdp"), None),
        P(("dp", "fsdp"), None),
        P(("dp", "fsdp"), None),
        P(("dp", "fsdp"), None),
        P(("dp", "fsdp")),
        P(("dp", "fsdp"), None),
        P(("dp", "fsdp"), None),
        P(("dp", "fsdp"), None),
        P(("dp", "fsdp"), None),
        P(("dp", "fsdp")),
        P(("dp", "fsdp"), None),
        P(("dp", "fsdp"), None),
    )
    out_specs = (
        P(("dp", "fsdp"), None),
        P(("dp", "fsdp"), None),
        P(("dp", "fsdp"), None, None),
        P(None, ("dp", "fsdp")),
        P(),
        P(("dp", "fsdp")),
        P(("dp", "fsdp"), None),
        P(("dp", "fsdp"), None),
        P(("dp", "fsdp"), None),
        P(("dp", "fsdp"), None),
        P(("dp", "fsdp")),
        P(("dp", "fsdp"), None),
        P(("dp", "fsdp"), None),
        P(("dp", "fsdp"), None),
        P(("dp", "fsdp"), None),
        P(("dp", "fsdp")),
        P(("dp", "fsdp"), None),
        P(("dp", "fsdp"), None),
    )
    return jax.shard_map(local, mesh=mesh, in_specs=in_specs, out_specs=out_specs, check_vma=False)
```

profile of v0, /device:TPU:0, one launch (start us, length us, event | category | flops | bytes accessed | tf_op | source)
XLA Modules:
  0.0 1728.8 jit_solution(16612811108382737713)
XLA Ops:
  16.6 42.0 %all-reduce.8 = (bf16[768]{0:T(1024)(128)(2,1)S(1)}, bf16[768]{0:T(1024)(128)(2,1)S(1)}, bf16[768]{0:T(1024)(128)(2,1)S(1)}) all-reduce(bf16[768]{0:T(1024)(128)(2,1)S(1)} %dynamic-update-slice, bf16[768]{0:T(1024)(128)(2,1)S(1)} %dynamic-update-slice.1, ...), channel_id=1, replica_groups=mesh['dp'=4,'fsdp'=8] {'dp','fsdp'}, use_global_device_ids=true, to_apply=%add | all-reduce | flops 2304 | bytes 9216
  58.6 66.5 %all-gather = bf16[32,24,8]{1,2,0:T(8,128)(2,1)S(1)} all-gather(bf16[1,24,8]{1,2,0:T(8,128)(2,1)} %bitcast.213), channel_id=1, replica_groups=mesh['dp'=4,'fsdp'=8] {'dp','fsdp'}, dimensions={0}, use_global_device_ids=true | all-gather | bytes 12672 | tf_op jit(solution)/shard_map/all_gather | solution.py:129
  125.3 4.7 select_bitcast_fusion
  130.0 4.9 copy.120
  146.9 33.3 %all-gather.12.cloned.1.call-done = bf16[768,768]{1,0:T(8,128)(2,1)} async-done(((bf16[24,768]{1,0:T(8,128)(2,1)}), bf16[768,768]{1,0:T(8,128)(2,1)}) %all-gather.12.cloned.1.call-update) | async-done | bytes 1179664 | tf_op jit(solution)/shard_map/all_gather | solution.py:132
  182.8 53.4 %all-gather.20.cloned.1.call-done = bf16[768,768]{1,0:T(8,128)(2,1)} async-done(((bf16[24,768]{1,0:T(8,128)(2,1)}), bf16[768,768]{1,0:T(8,128)(2,1)}) %all-gather.20.cloned.1.call-update) | async-done | bytes 1179664 | tf_op jit(solution)/shard_map/all_gather | solution.py:174
  238.9 3.3 convolution_convert_fusion.3
  242.2 4.9 copy.126
  247.1 45.1 %all-gather.24.cloned.1.call-done = bf16[768,768]{1,0:T(8,128)(2,1)} async-done(((bf16[24,768]{1,0:T(8,128)(2,1)}), bf16[768,768]{1,0:T(8,128)(2,1)}) %all-gather.24.cloned.1.call-update) | async-done | bytes 1179664 | tf_op jit(solution)/shard_map/all_gather | solution.py:173
  294.8 3.3 convolution_convert_fusion.2
  298.1 5.2 copy.130
  303.3 3.3 add_reduce_fusion
  314.1 34.1 %all-gather.18.cloned.1.call-done = bf16[768,768]{1,0:T(8,128)(2,1)} async-done(((bf16[24,768]{1,0:T(8,128)(2,1)}), bf16[768,768]{1,0:T(8,128)(2,1)}) %all-gather.18.cloned.1.call-update) | async-done | bytes 1179664 | tf_op jit(solution)/shard_map/all_gather | solution.py:133
  350.8 53.4 %all-gather.22.cloned.1.call-done = bf16[768,768]{1,0:T(8,128)(2,1)} async-done(((bf16[24,768]{1,0:T(8,128)(2,1)}), bf16[768,768]{1,0:T(8,128)(2,1)}) %all-gather.22.cloned.1.call-update) | async-done | bytes 1179664 | tf_op jit(solution)/shard_map/all_gather | solution.py:172
  412.4 3.6 fusion.81
  420.7 3.6 fusion.27
  426.2 34.2 %all-gather.26.cloned.1.call-done = bf16[768,768]{1,0:T(8,128)(2,1)} async-done(((bf16[24,768]{1,0:T(8,128)(2,1)}), bf16[768,768]{1,0:T(8,128)(2,1)}) %all-gather.26.cloned.1.call-update) | async-done | bytes 1179664 | tf_op jit(solution)/shard_map/all_gather | solution.py:175
  460.4 3.5 multiply_reduce_fusion.8
  463.9 62.2 %all-gather.30.cloned.1.call-done = bf16[3072,768]{1,0:T(8,128)(2,1)} async-done(((bf16[96,768]{1,0:T(8,128)(2,1)}), bf16[3072,768]{1,0:T(8,128)(2,1)}) %all-gather.30.cloned.1.call-update) | async-done | bytes 4718608 | tf_op jit(solution)/shard_map/all_gather | solution.py:207
  526.0 7.9 fusion.82
  533.9 57.5 %all-gather.28.cloned.1.call-done = bf16[768,3072]{1,0:T(8,128)(2,1)} async-done(((bf16[24,3072]{1,0:T(8,128)(2,1)}), bf16[768,3072]{1,0:T(8,128)(2,1)}) %all-gather.28.cloned.1.call-update) | async-done | bytes 4718608 | tf_op jit(solution)/shard_map/all_gather | solution.py:206
  591.4 12.1 fusion.9
  610.4 3.4 convolution_convert_fusion.10
  619.2 8.7 fusion.13
  627.9 5.9 copy.152
  633.8 7.8 convolution_convert_fusion
  648.8 7.9 multiply_reduce_fusion
  656.7 6.7 multiply_convert_fusion
  678.0 5.6 fusion.42
  683.6 6.2 copy.149
  689.9 7.8 convolution_convert_fusion.1
  719.8 5.4 multiply_reduce_fusion.1
  725.3 6.3 convert_reduce_fusion
  746.7 9.7 fusion.79
  757.8 7.3 fusion.75
  769.4 5.2 copy.154
  783.2 4.4 fusion.35
  787.6 41.2 %all-reduce.7 = (f32[8,768]{1,0:T(8,128)S(1)}, f32[32,12]{0,1:T(8,128)}, f32[768]{0:T(1024)S(1)}, f32[768]{0:T(1024)S(1)}, f32[768]{0:T(1024)S(1)}) all-reduce(f32[8,768]{1,0:T(8,128)S(1)} %fusion.65, f32[32,12]{0,1:T(8,128)S(1)} %fusion.35, f32[768]{0:T(1024)S(1)} %get-tuple-element.175, ...), channel_id=2, replica_groups=mesh['dp'=4,'fsdp'=8] {'dp','fsdp'}, use_global_device_ids=true, to_apply=%region_13.14.clone | all-reduce | flops 8832 | bytes 70656
  831.2 3.4 fusion.85
  837.7 8.9 add_convert_fusion
  846.6 70.4 %reduce-scatter.24.cloned.1.call-done = f32[24,768]{1,0:T(8,128)} async-done(((f32[768,768]{1,0:T(8,128)}), f32[24,768]{1,0:T(8,128)}) %reduce-scatter.24.cloned.1.call-update) | async-done | bytes 73744 | tf_op jit(solution)/shard_map/reduce_scatter | solution.py:294
  917.0 104.7 %reduce-scatter.22.cloned.1.call-done = f32[24,768]{1,0:T(8,128)} async-done(((f32[768,768]{1,0:T(8,128)}), f32[24,768]{1,0:T(8,128)}) %reduce-scatter.22.cloned.1.call-update) | async-done | bytes 73744 | tf_op jit(solution)/shard_map/reduce_scatter | solution.py:357
  1021.7 103.8 %reduce-scatter.32.cloned.1.call-done = f32[24,768]{1,0:T(8,128)} async-done(((f32[768,768]{1,0:T(8,128)}), f32[24,768]{1,0:T(8,128)}) %reduce-scatter.32.cloned.1.call-update) | async-done | bytes 73744
  1125.4 104.7 %reduce-scatter.20.cloned.1.call-done = f32[24,768]{1,0:T(8,128)} async-done(((f32[768,768]{1,0:T(8,128)}), f32[24,768]{1,0:T(8,128)}) %reduce-scatter.20.cloned.1.call-update) | async-done | bytes 73744 | tf_op jit(solution)/shard_map/reduce_scatter | solution.py:356
  1230.1 103.8 %reduce-scatter.16.cloned.1.call-done = f32[24,768]{1,0:T(8,128)} async-done(((f32[768,768]{1,0:T(8,128)}), f32[24,768]{1,0:T(8,128)}) %reduce-scatter.16.cloned.1.call-update) | async-done | bytes 73744 | tf_op jit(solution)/shard_map/reduce_scatter | solution.py:354
  1333.9 104.7 %reduce-scatter.18.cloned.1.call-done = f32[24,768]{1,0:T(8,128)} async-done(((f32[768,768]{1,0:T(8,128)}), f32[24,768]{1,0:T(8,128)}) %reduce-scatter.18.cloned.1.call-update) | async-done | bytes 73744 | tf_op jit(solution)/shard_map/reduce_scatter | solution.py:355
  1438.6 141.1 %reduce-scatter.30.cloned.1.call-done = f32[96,768]{1,0:T(8,128)} async-done(((f32[3072,768]{1,0:T(8,128)}), f32[96,768]{1,0:T(8,128)}) %reduce-scatter.30.cloned.1.call-update) | async-done | bytes 294928 | tf_op jit(solution)/shard_map/reduce_scatter | solution.py:231
  1579.7 141.8 %reduce-scatter.28.cloned.1.call-done = f32[24,3072]{1,0:T(8,128)} async-done(((f32[768,3072]{1,0:T(8,128)}), f32[24,3072]{1,0:T(8,128)}) %reduce-scatter.28.cloned.1.call-update) | async-done | bytes 294928 | tf_op jit(solution)/shard_map/reduce_scatter | solution.py:230
  (249 shorter events, 144.4 us)
Async XLA Ops:
  7.2 229.0 %copy-start = (bf16[2,512,768]{2,1,0:T(8,128)(2,1)S(1)}, bf16[2,512,768]{2,1,0:T(8,128)(2,1)}, u32[]{:S(2)}) copy-start(bf16[2,512,768]{2,1,0:T(8,128)(2,1)} %param.23) | copy-start | bytes 4718596
  7.2 128.6 %all-gather.16.cloned.1.call-start = ((), (), s32[]{:S(2)}) async-start(), calls=%async_computation.12 | async-start | bytes 1216512 | tf_op jit(solution)/shard_map/all_gather | solution.py:131
  7.9 133.5 %all-gather.14.cloned.1.call-start = ((), (), s32[]{:S(2)}) async-start(), calls=%async_computation.11 | async-start | bytes 1216512 | tf_op jit(solution)/shard_map/all_gather | solution.py:130
  8.7 171.5 %all-gather.12.cloned.1.call-start = ((), (), s32[]{:S(2)}) async-start(), calls=%async_computation.10 | async-start | bytes 1216512 | tf_op jit(solution)/shard_map/all_gather | solution.py:132
  9.4 226.8 %all-gather.20.cloned.1.call-start = ((), (), s32[]{:S(2)}) async-start(), calls=%async_computation.14 | async-start | bytes 1216512 | tf_op jit(solution)/shard_map/all_gather | solution.py:174
  10.0 282.2 %all-gather.24.cloned.1.call-start = ((), (), s32[]{:S(2)}) async-start(), calls=%async_computation.16 | async-start | bytes 1216512 | tf_op jit(solution)/shard_map/all_gather | solution.py:173
  10.6 337.5 %all-gather.18.cloned.1.call-start = ((), (), s32[]{:S(2)}) async-start(), calls=%async_computation.13 | async-start | bytes 1216512 | tf_op jit(solution)/shard_map/all_gather | solution.py:133
  11.2 393.1 %all-gather.22.cloned.1.call-start = ((), (), s32[]{:S(2)}) async-start(), calls=%async_computation.15 | async-start | bytes 1216512 | tf_op jit(solution)/shard_map/all_gather | solution.py:172
  11.9 448.5 %all-gather.26.cloned.1.call-start = ((), (), s32[]{:S(2)}) async-start(), calls=%async_computation.17 | async-start | bytes 1216512 | tf_op jit(solution)/shard_map/all_gather | solution.py:175
  12.7 513.4 %all-gather.30.cloned.1.call-start = ((), (), s32[]{:S(2)}) async-start(), calls=%async_computation.19 | async-start | bytes 4866048 | tf_op jit(solution)/shard_map/all_gather | solution.py:207
  13.4 578.0 %all-gather.28.cloned.1.call-start = ((), (), s32[]{:S(2)}) async-start(), calls=%async_computation.18 | async-start | bytes 4866048 | tf_op jit(solution)/shard_map/all_gather | solution.py:206
  14.0 832.6 %reduce-scatter.26.cloned.1.call-start = ((), (), s32[]{:S(2)}) async-start(), calls=%async_computation.25 | async-start | bytes 2433024 | tf_op jit(solution)/shard_map/reduce_scatter | solution.py:297
  58.6 76.8 %copy-start.47 = (f32[768]{0:T(1024)}, f32[768]{0:T(1024)S(1)}, u32[]{:S(2)}) copy-start(f32[768]{0:T(1024)S(1)} %convert_element_type.171) | copy-start | bytes 9220
  130.0 5.0 copy-start.56
  130.0 5.1 copy-start.8
  135.4 3.5 copy-start.51
  135.5 3.5 copy-start.49
  135.7 44.5 %copy-start.20 = (bf16[512,768]{1,0:T(8,128)(2,1)}, bf16[512,768]{1,0:T(8,128)(2,1)S(1)}, u32[]{:S(2)}) copy-start(bf16[512,768]{1,0:T(8,128)(2,1)S(1)} %multiply_convert_fusion.5) | copy-start | bytes 2359300
  182.8 127.8 %copy-start.22 = (bf16[2,256,12,64]{1,0,3,2:T(2,128)(2,1)}, bf16[2,256,12,64]{1,0,3,2:T(2,128)(2,1)S(1)}, u32[]{:S(2)}) copy-start(bf16[2,256,12,64]{1,0,3,2:T(2,128)(2,1)S(1)} %reshape.295) | copy-start | bytes 2359300
  236.2 2.7 copy-start.55
  298.1 5.2 copy-start.26
  303.3 3.4 copy-start.2
  306.6 2.6 copy-start.4
  416.0 4.7 copy-start.1
  416.0 4.7 copy-start.19
  591.4 12.1 copy-start.11
  591.4 12.1 copy-start.53
  603.5 2.9 copy-start.35
  603.5 2.9 copy-start.45
  610.3 236.3 %reduce-scatter.34.cloned.1.call-start = ((), (), s32[]{:S(2)}) async-start(), calls=%async_computation.29 | async-start | bytes 2433024
  648.7 268.3 %reduce-scatter.24.cloned.1.call-start = ((), (), s32[]{:S(2)}) async-start(), calls=%async_computation.24 | async-start | bytes 2433024 | tf_op jit(solution)/shard_map/reduce_scatter | solution.py:294
  656.7 6.7 copy-start.13
  663.4 2.7 copy-start.5
  670.3 351.4 %reduce-scatter.22.cloned.1.call-start = ((), (), s32[]{:S(2)}) async-start(), calls=%async_computation.23 | async-start | bytes 2433024 | tf_op jit(solution)/shard_map/reduce_scatter | solution.py:357
  670.3 2.8 copy-start.18
  676.9 448.6 %reduce-scatter.32.cloned.1.call-start = ((), (), s32[]{:S(2)}) async-start(), calls=%async_computation.28 | async-start | bytes 2433024
  704.7 525.4 %reduce-scatter.20.cloned.1.call-start = ((), (), s32[]{:S(2)}) async-start(), calls=%async_computation.22 | async-start | bytes 2433024 | tf_op jit(solution)/shard_map/reduce_scatter | solution.py:356
  718.7 615.2 %reduce-scatter.16.cloned.1.call-start = ((), (), s32[]{:S(2)}) async-start(), calls=%async_computation.20 | async-start | bytes 2433024 | tf_op jit(solution)/shard_map/reduce_scatter | solution.py:354
  719.8 5.5 copy-start.3
  725.3 6.4 copy-start.28
  737.3 701.3 %reduce-scatter.18.cloned.1.call-start = ((), (), s32[]{:S(2)}) async-start(), calls=%async_computation.21 | async-start | bytes 2433024 | tf_op jit(solution)/shard_map/reduce_scatter | solution.py:355
  745.6 834.1 %reduce-scatter.30.cloned.1.call-start = ((), (), s32[]{:S(2)}) async-start(), calls=%async_computation.27 | async-start | bytes 9732096 | tf_op jit(solution)/shard_map/reduce_scatter | solution.py:231
  756.5 965.0 %reduce-scatter.28.cloned.1.call-start = ((), (), s32[]{:S(2)}) async-start(), calls=%async_computation.26 | async-start | bytes 9732096 | tf_op jit(solution)/shard_map/reduce_scatter | solution.py:230
  765.2 2.9 copy-start.41
  780.3 2.8 copy-start.10
  780.3 2.8 copy-start.44
  831.2 3.4 copy-start.33
  831.2 3.4 copy-start.42
  (30 other events, 41.8 us)
Sparse Core Ops, SparseCore 0:
  11.0 56.8 all-gather.15
  70.9 53.1 all-gather.13
  127.1 53.0 all-gather.11
  183.1 53.0 all-gather.19
  239.0 53.0 all-gather.23
  295.0 53.0 all-gather.17
  351.1 53.0 all-gather.21
  407.2 53.1 all-gather.25
  463.4 62.6 all-gather.29
  528.9 62.4 all-gather.27
  610.4 97.8 reduce-scatter.25
  714.8 98.1 reduce-scatter.33
  818.9 98.0 reduce-scatter.23
  923.6 98.0 reduce-scatter.21
  1027.4 98.0 reduce-scatter.31
  1132.0 98.0 reduce-scatter.19
  1235.8 97.9 reduce-scatter.15
  1340.5 98.0 reduce-scatter.17
  1445.1 134.5 reduce-scatter.29
  1587.0 134.4 reduce-scatter.27
where the time goes:
time: 1740 us; the launch traced here: 1730 us
  waiting for transfers between devices  1250 us (72%)
  matrix products  190 us (11%)
  blocking collectives  150 us (9%)
  local copies, waits for them, and re-layouts  96.8 us (6%)
  other arithmetic  21.7 us (1%)
    reduce_scatter x1, waiting for transfers between devices, local(): lax.psum_scatter(inner_full, ('dp', 'fsdp'), scatter_dimension=0, tiled=T...  142 us
    reduce_scatter x1, waiting for transfers between devices, local(): lax.psum_scatter(outer_full, ('dp', 'fsdp'), scatter_dimension=0, tiled=T...  141 us
    unnamed x22, waiting for transfers between devices  110 us
    reduce_scatter x1, waiting for transfers between devices, local(): lax.psum_scatter(key_full, ('dp', 'fsdp'), scatter_dimension=0, tiled=True)  105 us
    reduce_scatter x1, waiting for transfers between devices, local(): lax.psum_scatter(value_full, ('dp', 'fsdp'), scatter_dimension=0, tiled=T...  105 us
    reduce_scatter x1, waiting for transfers between devices, local(): lax.psum_scatter(out_full, ('dp', 'fsdp'), scatter_dimension=0, tiled=True)  105 us
    reduce_scatter x1, waiting for transfers between devices, local(): lax.psum_scatter(query_full, ('dp', 'fsdp'), scatter_dimension=0, tiled=T...  104 us
    unnamed x2, blocking collectives  83.2 us
  transfers between devices with their start and end apart: 20, of which 16 were waited for; matrix products, arithmetic and copies ran while one was open for 15% of the time, Pallas kernels for 0%

commit v1 on v0

--- a/solution.py
+++ b/solution.py
@@ -1,6 +1,10 @@
+import functools
+
 import jax
 import jax.numpy as jnp
 from jax import lax
+from jax.experimental import pallas as pl
+from jax.experimental.pallas import tpu as pltpu
 from jax.sharding import PartitionSpec as P
 
 H = 12
@@ -90,7 +94,483 @@
     return grads
 
 
+MESH = pl.DeviceIdType.MESH
+ALL = slice(None)
+
+
+class Place:
+    def __init__(self, sizes):
+        self.ny, self.nz = sizes
+        self.dp = lax.axis_index("dp")
+        self.fs = lax.axis_index("fsdp")
+        self.c, self.y = lax.rem(self.dp, 2), lax.div(self.dp, 2)
+        self.x, self.z = lax.rem(self.fs, 2), lax.div(self.fs, 2)
+
+    def size(self, dim):
+        return {"c": 2, "x": 2, "y": self.ny, "z": self.nz}[dim]
+
+    def at(self, dim):
+        return {"c": self.c, "x": self.x, "y": self.y, "z": self.z}[dim]
+
+    def device(self, dim, index):
+        if dim == "c":
+            return (self.y * 2 + index, self.fs)
+        if dim == "y":
+            return (index * 2 + self.c, self.fs)
+        if dim == "x":
+            return (self.dp, self.z * 2 + index)
+        return (self.dp, index * 2 + self.x)
+
+
+def neighbour_barrier(place, far=False):
+    barrier = pltpu.get_barrier_semaphore()
+    links = []
+    for dim in "cxyz":
+        here, size = place.at(dim), place.size(dim)
+        reach = 1
+        while reach < size and (reach == 1 or far):
+            if size == 2:
+                links.append((dim, 1 - here, None))
+            elif reach == 1:
+                for step in (1, -1):
+                    links.append((dim, here + step, (here + step >= 0) & (here + step < size)))
+            else:
+                links.append((dim, here + reach - 2 * reach * lax.rem(lax.div(here, reach), 2), None))
+            reach *= 2
+
+    def signal(dim, there):
+        pl.semaphore_signal(barrier, inc=1, device_id=place.device(dim, there), device_id_type=MESH)
+
+    for dim, there, condition in links:
+        if condition is None:
+            signal(dim, there)
+        else:
+            pl.when(condition)(lambda dim=dim, there=there: signal(dim, there))
+    peers = sum(1 if condition is None else condition.astype(jnp.int32) for _, _, condition in links)
+    pl.semaphore_wait(barrier, peers)
+
+
+PATHS = ("zxy", "zyx", "xzy", "yzx")
+
+
+class Link:
+    def __init__(self, copy, sends=None, receives=None):
+        self.copy, self.sends, self.receives = copy, sends, receives
+
+    @staticmethod
+    def when(condition, run):
+        if condition is None:
+            run()
+        else:
+            pl.when(condition)(run)
+
+    def start(self):
+        self.when(self.sends, lambda: self.copy.start())
+
+    def wait_send(self):
+        self.when(self.sends, lambda: self.copy.wait_send())
+
+    def wait_recv(self):
+        self.when(self.receives, lambda: self.copy.wait_recv())
+
+
+def pick(held, place, **fixed):
+    return tuple(fixed.get(dim, ALL if dim in held else place.at(dim)) for dim in "yczx")
+
+
+def gather_steps(place, blocks, path, sems):
+    steps, slot, held = [], 0, ""
+    for dim in path + "c":
+        here, size = place.at(dim), place.size(dim)
+        if size == 2:
+            there = 1 - here
+            index = pick(held, place)
+            copy = pltpu.make_async_remote_copy(
+                blocks(index), blocks(index), sems[0].at[slot], sems[1].at[slot],
+                device_id=place.device(dim, there), device_id_type=MESH,
+            )
+            steps.append([Link(copy)])
+            slot += 1
+        else:
+            for hop in range(1, size):
+                links = []
+                for way in (1, -1):
+                    origin = here - way * (hop - 1)
+                    there = here + way
+                    source = here - way * hop
+                    index = pick(held, place, **{dim: jnp.clip(origin, 0, size - 1)})
+                    copy = pltpu.make_async_remote_copy(
+                        blocks(index), blocks(index), sems[0].at[slot], sems[1].at[slot],
+                        device_id=place.device(dim, jnp.clip(there, 0, size - 1)), device_id_type=MESH,
+                    )
+                    sends = (origin >= 0) & (origin < size) & (there >= 0) & (there < size)
+                    links.append(Link(copy, sends, (source >= 0) & (source < size)))
+                    slot += 1
+                steps.append(links)
+        held += dim
+    return steps
+
+
+def slot_count(sizes):
+    ny, nz = sizes
+    return 2 + (1 if ny == 2 else 2 * (ny - 1)) + (1 if nz == 2 else 2 * (nz - 1))
+
+
+def run_steps(plans, lag):
+    rounds = max(lag[i] + len(plan) for i, plan in enumerate(plans)) + 1
+    for now in range(rounds):
+        for offset, plan in zip(lag, plans):
+            at = now - offset
+            if 1 <= at <= len(plan):
+                for link in plan[at - 1]:
+                    link.wait_recv()
+            if 0 <= at < len(plan):
+                for link in plan[at]:
+                    link.start()
+    for plan in plans:
+        for links in plan:
+            for link in links:
+                link.wait_send()
+
+
+def gather_kernel(sizes, *refs):
+    shards, wholes = refs[:11], refs[11:22]
+    own_sem, send_sem, recv_sem = refs[22:]
+    place = Place(sizes)
+    own = (place.y, place.c, place.z, place.x)
+    owns = [
+        pltpu.make_async_copy(shard, whole.at[own], own_sem.at[i])
+        for i, (shard, whole) in enumerate(zip(shards, wholes))
+    ]
+    for copy in owns:
+        copy.start()
+    neighbour_barrier(place)
+    views = [lambda index, ref=ref: ref.at[index] for ref in wholes[:9]]
+    width = wholes[8].shape[-1]
+    for q in range(4):
+        views.append(
+            lambda index, q=q: wholes[9].at[index + (ALL, pl.ds(q * width, width))]
+        )
+    for q in range(4):
+        views.append(lambda index, q=q: wholes[10].at[index + (q,)])
+    plans, lag = [], []
+    for i, view in enumerate(views):
+        path = PATHS[0] if i == 0 else PATHS[(i - 1) % 4]
+        plans.append(gather_steps(place, view, path, (send_sem.at[i], recv_sem.at[i])))
+        lag.append(0 if i == 0 else 3 * ((i - 1) // 4))
+    for copy in owns:
+        copy.wait()
+    run_steps(plans, lag)
+
+
+def gather_weights(sizes, table, gains, squares, inner, outer):
+    ny, nz = sizes
+    grid = (ny, 2, nz, 2)
+    part, width = squares[0].shape
+    small = jnp.zeros((16, 128), table.dtype)
+    small = small.at[: table.shape[0], :part].set(table)
+    for i, gain in enumerate(gains):
+        small = small.at[table.shape[0] + i, :part].set(gain)
+    shards = (small,) + tuple(squares) + (inner, outer.reshape(4, part, width))
+    anywhere = pl.BlockSpec(memory_space=pl.ANY)
+    slots = slot_count(sizes)
+    wholes = pl.pallas_call(
+        functools.partial(gather_kernel, sizes),
+        out_shape=[jax.ShapeDtypeStruct(grid + s.shape, s.dtype) for s in shards],
+        in_specs=[anywhere] * 11,
+        out_specs=[anywhere] * 11,
+        scratch_shapes=[
+            pltpu.SemaphoreType.DMA((11,)),
+            pltpu.SemaphoreType.DMA((17, slots)),
+            pltpu.SemaphoreType.DMA((17, slots)),
+        ],
+        compiler_params=pltpu.CompilerParams(collective_id=0, has_side_effects=True),
+    )(*shards)
+    count = ny * nz * 4
+    tiny = wholes[0].reshape(count, 16, 128)[:, :, :part].transpose(1, 0, 2).reshape(16, count * part)
+    rows = table.shape[0]
+    return (
+        (tiny[rows], tiny[rows + 1], tiny[rows + 2], tiny[:rows])
+        + tuple(w.reshape(count * part, width) for w in wholes[1:9])
+        + (wholes[9].reshape(count * part, 4 * width), wholes[10].reshape(4 * count * part, width))
+    )
+
+
+class Reduce:
+    def __init__(self, place, path, source, total, core_in, boxes, out, sems):
+        self.place, self.path, self.source, self.total = place, path, source, total
+        self.core_in, self.boxes, self.out, self.sems = core_in, boxes, out, sems
+        self.slot = 0
+        self.sent = []
+
+    def copy(self, source, target, dim, there):
+        slot = self.slot
+        self.slot += 1
+        return pltpu.make_async_remote_copy(
+            source, target, self.sems[0].at[slot], self.sems[1].at[slot],
+            device_id=self.place.device(dim, there), device_id_type=MESH,
+        )
+
+    def index(self, fixed):
+        return tuple(fixed.get(dim, ALL) for dim in "yzx")
+
+    def add(self, target, box):
+        shape = box.shape[:-2]
+        count = 1
+        for size in shape:
+            count *= size
+        free = [i for i, entry in enumerate(target) if entry is ALL]
+
+        def body(n, _):
+            spots, rest = [], n
+            for size in reversed(shape):
+                spots.append(lax.rem(rest, size))
+                rest = lax.div(rest, size)
+            spots = spots[::-1]
+            full = list(target)
+            for place_at, spot in zip(free, spots):
+                full[place_at] = spot
+            mine = self.total[tuple(full)].astype(jnp.float32)
+            got = box[tuple(spots)].astype(jnp.float32)
+            self.total[tuple(full)] = (mine + got).astype(jnp.bfloat16)
+            return 0
+
+        if count == 1:
+            body(0, 0)
+        else:
+            lax.fori_loop(0, count, body, 0)
+
+    def steps(self):
+        place, listing = self.place, []
+        own = pltpu.make_async_copy(self.source(place.c), self.total, self.sems[2])
+        core = self.copy(self.source(1 - place.c), self.core_in, "c", 1 - place.c)
+
+        def start():
+            own.start()
+            core.start()
+
+        def finish():
+            own.wait()
+            core.wait_recv()
+            self.add((ALL, ALL, ALL), self.core_in)
+
+        self.sent.append(Link(core))
+        listing.append((start, finish))
+        fixed, box = {}, 0
+        for dim in self.path:
+            here, size = place.at(dim), place.size(dim)
+            if size == 2:
+                target = self.index({**fixed, dim: 1 - here})
+                link = Link(self.copy(self.total.at[target], self.boxes[box], dim, 1 - here))
+                self.sent.append(link)
+                listing.append(self.pair([link], [(self.index({**fixed, dim: here}), box, None)]))
+                box += 1
+            else:
+                for hop in range(size - 1, 0, -1):
+                    links, adds = [], []
+                    for way in (1, -1):
+                        there = here - way
+                        goal = here - way * hop
+                        sends = (goal >= 0) & (goal < size)
+                        source = here + way
+                        got = source - way * hop
+                        receives = (source >= 0) & (source < size) & (got >= 0) & (got < size)
+                        target = self.index({**fixed, dim: jnp.clip(goal, 0, size - 1)})
+                        copy = self.copy(
+                            self.total.at[target], self.boxes[box], dim, jnp.clip(there, 0, size - 1)
+                        )
+                        link = Link(copy, sends, receives)
+                        self.sent.append(link)
+                        links.append(link)
+                        adds.append((self.index({**fixed, dim: jnp.clip(got, 0, size - 1)}), box, receives))
+                        box += 1
+                    listing.append(self.pair(links, adds))
+            fixed = {**fixed, dim: here}
+        return listing
+
+    def pair(self, links, adds):
+        def start():
+            for link in links:
+                link.start()
+
+        def finish():
+            for link in links:
+                link.wait_recv()
+            for target, box, condition in adds:
+                Link.when(condition, functools.partial(self.add, target, self.boxes[box]))
+
+        return start, finish
+
+    def close(self):
+        own = (self.place.y, self.place.z, self.place.x)
+        self.out(self.total[own].astype(jnp.float32))
+        for link in self.sent:
+            link.wait_send()
+
+
+def box_shapes(sizes, path):
+    ny, nz = sizes
+    size = {"y": ny, "z": nz, "x": 2}
+    left, shapes = "yzx", []
+    for dim in path:
+        left = left.replace(dim, "")
+        lead = tuple(size[d] for d in left)
+        shapes += [lead] * (1 if size[dim] == 2 else 2 * (size[dim] - 1))
+    return shapes
+
+
+BACK_PATHS = tuple(path[::-1] for path in PATHS)
+
+
+def reduce_kernel(sizes, box_counts, *refs):
+    sources, small_in = refs[:10], refs[10]
+    outs, small_out = refs[11:21], refs[21]
+    totals, core_boxes = refs[22], refs[23]
+    at = 24
+    boxes = []
+    for count in box_counts:
+        boxes.append(refs[at : at + count])
+        at += count
+    small_box, own_sem, send_sem, recv_sem, small_send, small_recv = refs[at:]
+    place = Place(sizes)
+    neighbour_barrier(place, far=True)
+    width = outs[0].shape[-1]
+
+    def square(ref):
+        return lambda core: ref.at[:, core]
+
+    def inner(q):
+        return lambda core: sources[8].at[:, core, :, :, :, pl.ds(q * width, width)]
+
+    def outer(q):
+        return lambda core: sources[9].at[:, core, :, :, q]
+
+    views = [inner(q) for q in range(4)] + [outer(q) for q in range(4)]
+    views += [square(sources[i]) for i in (4, 5, 6, 7, 0, 1, 2, 3)]
+
+    def store_square(i):
+        def run(value):
+            outs[i][...] = value
+
+        return run
+
+    def store_inner(q):
+        def run(value):
+            outs[8][:, q * width : (q + 1) * width] = value
+
+        return run
+
+    def store_outer(q):
+        def run(value):
+            outs[9][q] = value
+
+        return run
+
+    stores = [store_inner(q) for q in range(4)] + [store_outer(q) for q in range(4)]
+    stores += [store_square(i) for i in (4, 5, 6, 7, 0, 1, 2, 3)]
+    plans, lag = [], []
+    reduces = []
+    for m in range(16):
+        group, kind = m // 4, m % 4
+        reduce = Reduce(
+            place, BACK_PATHS[kind], views[m], totals.at[m], core_boxes.at[m],
+            [box.at[group] for box in boxes[kind]], stores[m],
+            (send_sem.at[m], recv_sem.at[m], own_sem.at[m]),
+        )
+        reduces.append(reduce)
+        plans.append(reduce.steps())
+        lag.append(3 * group)
+    small_out[...] = small_in[...]
+    small = []
+    moves = [("c", 1 - place.c), ("x", 1 - place.x), ("y", None), ("z", None)]
+    for dim, there in moves:
+        size, here, reach = place.size(dim), place.at(dim), 1
+        while reach < size:
+            partner = here + reach - 2 * reach * lax.rem(lax.div(here, reach), 2)
+            small.append((dim, partner))
+            reach *= 2
+    rounds = max(max(lag[i] + len(plan) for i, plan in enumerate(plans)) + 1, len(small) + 1)
+    copies = []
+    for now in range(rounds):
+        for offset, plan in zip(lag, plans):
+            step = now - offset
+            if 1 <= step <= len(plan):
+                plan[step - 1][1]()
+            if 0 <= step < len(plan):
+                plan[step][0]()
+        if 1 <= now <= len(small):
+            copies[-1].wait()
+            small_out[...] += small_box[now - 1]
+        if now < len(small):
+            dim, partner = small[now]
+            copies.append(
+                pltpu.make_async_remote_copy(
+                    small_out, small_box.at[now], small_send.at[now], small_recv.at[now],
+                    device_id=place.device(dim, partner), device_id_type=MESH,
+                )
+            )
+            copies[-1].start()
+    for reduce in reduces:
+        reduce.close()
+
+
+def reduce_grads(sizes, language, bucket, gains, squares, inner, outer):
+    ny, nz = sizes
+    grid = (ny, 2, nz, 2)
+    count = ny * nz * 4
+    width = squares[0].shape[1]
+    part = squares[0].shape[0] // count
+    langs = language.shape[0]
+    flat = jnp.zeros((width,), jnp.float32).at[: bucket.size].set(bucket.reshape(-1))
+    small = jnp.concatenate(
+        [language] + [g.reshape(1, width) for g in gains] + [flat[None], jnp.zeros((4, width), jnp.float32)], axis=0
+    )
+    sources = [to_low(s).reshape(grid + (part, width)) for s in squares]
+    sources += [
+        to_low(inner).reshape(grid + (part, 4 * width)),
+        to_low(outer).reshape(grid + (4, part, width)),
+    ]
+    anywhere = pl.BlockSpec(memory_space=pl.ANY)
+    vmem = pl.BlockSpec(memory_space=pltpu.VMEM)
+    shapes = [(part, width)] * 8 + [(part, 4 * width), (4, part, width), small.shape]
+    lead = [box_shapes(sizes, path) for path in BACK_PATHS]
+    slots = slot_count(sizes)
+    hops = (ny * nz * 4).bit_length() - 1
+    outs = pl.pallas_call(
+        functools.partial(reduce_kernel, sizes, tuple(len(s) for s in lead)),
+        out_shape=[jax.ShapeDtypeStruct(s, jnp.float32) for s in shapes],
+        in_specs=[anywhere] * 10 + [vmem],
+        out_specs=[vmem] * 11,
+        scratch_shapes=[
+            pltpu.VMEM((16, ny, nz, 2, part, width), jnp.bfloat16),
+            pltpu.VMEM((16, ny, nz, 2, part, width), jnp.bfloat16),
+        ]
+        + [pltpu.VMEM((4,) + s + (part, width), jnp.bfloat16) for one in lead for s in one]
+        + [
+            pltpu.VMEM((hops,) + small.shape, jnp.float32),
+            pltpu.SemaphoreType.DMA((16,)),
+            pltpu.SemaphoreType.DMA((16, slots)),
+            pltpu.SemaphoreType.DMA((16, slots)),
+            pltpu.SemaphoreType.DMA((hops,)),
+            pltpu.SemaphoreType.DMA((hops,)),
+        ],
+        compiler_params=pltpu.CompilerParams(
+            collective_id=1, has_side_effects=True, vmem_limit_bytes=60 * 1024 * 1024
+        ),
+    )(*sources, small)
+    start = (lax.axis_index("dp") * nz * 2 + lax.axis_index("fsdp")) * part
+    total = outs[10]
+    mine = lax.dynamic_slice(total, (0, start), (langs + 3, part))
+    return (
+        mine[:langs],
+        total[langs + 3, : bucket.size].reshape(bucket.shape),
+        mine[langs], mine[langs + 1], mine[langs + 2],
+        outs[:8], outs[8], outs[9].reshape(4 * part, width),
+    )
+
+
 def local(
+    sizes,
     hidden_in,
     output_grad,
     encoder_states,
@@ -120,18 +600,18 @@
     enc_length = encoder_states.shape[1]
     width = hidden_in.shape[1]
     blocks = seq_count // SEQ_BLOCK
+    (
+        gain_one, gain_two, gain_three, table_whole, query_whole, key_whole, value_whole, out_whole,
+        cquery_whole, ckey_whole, cvalue_whole, cout_whole, inner_whole, outer_whole,
+    ) = gather_weights(
+        sizes, language_table, (self_gain, cross_gain, feed_gain),
+        (self_query, self_key, self_value, self_out, cross_query, cross_key, cross_value, cross_out),
+        inner_weight, outer_weight,
+    )
 
     def to_blocks(array, rows):
         return array.reshape(blocks, SEQ_BLOCK, rows, array.shape[-1])
 
-    gain_one, table_whole, query_whole, key_whole, value_whole, out_whole = (
-        lax.all_gather(self_gain, ("dp", "fsdp"), axis=0, tiled=True),
-        lax.all_gather(language_table, ("dp", "fsdp"), axis=1, tiled=True),
-        lax.all_gather(self_query, ("dp", "fsdp"), axis=0, tiled=True),
-        lax.all_gather(self_key, ("dp", "fsdp"), axis=0, tiled=True),
-        lax.all_gather(self_value, ("dp", "fsdp"), axis=0, tiled=True),
-        lax.all_gather(self_out, ("dp", "fsdp"), axis=0, tiled=True),
-    )
     language_hot = (language_ids[:, None] == jnp.arange(table_whole.shape[0])[None, :]).astype(
         jnp.float32
     )
@@ -167,13 +647,6 @@
     )
     self_context = self_context.reshape(tokens, -1)
     mid_state = start_state + matmul(self_context, out_whole)
-    gain_two, cquery_whole, ckey_whole, cvalue_whole, cout_whole = (
-        lax.all_gather(cross_gain, ("dp", "fsdp"), axis=0, tiled=True),
-        lax.all_gather(cross_query, ("dp", "fsdp"), axis=0, tiled=True),
-        lax.all_gather(cross_key, ("dp", "fsdp"), axis=0, tiled=True),
-        lax.all_gather(cross_value, ("dp", "fsdp"), axis=0, tiled=True),
-        lax.all_gather(cross_out, ("dp", "fsdp"), axis=0, tiled=True),
-    )
     second_norm = to_low(norm_scale(mid_state, gain_two.astype(jnp.float32)))
     cross_queries = to_low(matmul(second_norm, cquery_whole))
     encoder_flat = encoder_states.reshape(enc_count * enc_length, width)
@@ -201,20 +674,10 @@
     )
     cross_context = cross_context.reshape(tokens, -1)
     late_state = mid_state + matmul(cross_context, cout_whole)
-    gain_three, inner_whole, outer_whole = (
-        lax.all_gather(feed_gain, ("dp", "fsdp"), axis=0, tiled=True),
-        lax.all_gather(inner_weight, ("dp", "fsdp"), axis=0, tiled=True),
-        lax.all_gather(outer_weight, ("dp", "fsdp"), axis=0, tiled=True),
-    )
     third_norm = to_low(norm_scale(late_state, gain_three.astype(jnp.float32)))
     expanded = matmul(third_norm, inner_whole)
     activated = to_low(jax.nn.gelu(expanded, approximate=True))
     hidden_out = (late_state + matmul(activated, outer_whole)).astype(jnp.bfloat16)
-    gain_three, inner_whole, outer_whole = (
-        lax.all_gather(feed_gain, ("dp", "fsdp"), axis=0, tiled=True),
-        lax.all_gather(inner_weight, ("dp", "fsdp"), axis=0, tiled=True),
-        lax.all_gather(outer_weight, ("dp", "fsdp"), axis=0, tiled=True),
-    )
     top_grad = output_grad.astype(jnp.float32)
     outer_full = left_product(activated, output_grad)
     activated_grad = right_product(output_grad, outer_whole)
@@ -225,18 +688,6 @@
     norm_value, norm_back = jax.vjp(norm_scale, late_state, gain_three.astype(jnp.float32))
     state_back, feed_gain_full = norm_back(third_grad)
     late_grad = top_grad + state_back
-    feed_gain_part, inner_part, outer_part = (
-        lax.psum_scatter(feed_gain_full, ("dp", "fsdp"), scatter_dimension=0, tiled=True),
-        lax.psum_scatter(inner_full, ("dp", "fsdp"), scatter_dimension=0, tiled=True),
-        lax.psum_scatter(outer_full, ("dp", "fsdp"), scatter_dimension=0, tiled=True),
-    )
-    gain_two, cquery_whole, ckey_whole, cvalue_whole, cout_whole = (
-        lax.all_gather(cross_gain, ("dp", "fsdp"), axis=0, tiled=True),
-        lax.all_gather(cross_query, ("dp", "fsdp"), axis=0, tiled=True),
-        lax.all_gather(cross_key, ("dp", "fsdp"), axis=0, tiled=True),
-        lax.all_gather(cross_value, ("dp", "fsdp"), axis=0, tiled=True),
-        lax.all_gather(cross_out, ("dp", "fsdp"), axis=0, tiled=True),
-    )
     cross_low = to_low(late_grad)
     cout_full = left_product(cross_context, cross_low)
     cross_context_grad = to_low(right_product(cross_low, cout_whole))
@@ -289,20 +740,6 @@
     norm_value, norm_back = jax.vjp(norm_scale, mid_state, gain_two.astype(jnp.float32))
     state_back, cross_gain_full = norm_back(second_grad)
     mid_grad = late_grad + state_back
-    cgain_part, cquery_part_sum, ckey_part_sum, cvalue_part_sum, cout_part = (
-        lax.psum_scatter(cross_gain_full, ("dp", "fsdp"), scatter_dimension=0, tiled=True),
-        lax.psum_scatter(cquery_full, ("dp", "fsdp"), scatter_dimension=0, tiled=True),
-        lax.psum_scatter(ckey_full, ("dp", "fsdp"), scatter_dimension=0, tiled=True),
-        lax.psum_scatter(cvalue_full, ("dp", "fsdp"), scatter_dimension=0, tiled=True),
-        lax.psum_scatter(cout_full, ("dp", "fsdp"), scatter_dimension=0, tiled=True),
-    )
-    gain_one, query_whole, key_whole, value_whole, out_whole = (
-        lax.all_gather(self_gain, ("dp", "fsdp"), axis=0, tiled=True),
-        lax.all_gather(self_query, ("dp", "fsdp"), axis=0, tiled=True),
-        lax.all_gather(self_key, ("dp", "fsdp"), axis=0, tiled=True),
-        lax.all_gather(self_value, ("dp", "fsdp"), axis=0, tiled=True),
-        lax.all_gather(self_out, ("dp", "fsdp"), axis=0, tiled=True),
-    )
     self_low = to_low(mid_grad)
     out_full = left_product(self_context, self_low)
     self_context_grad = to_low(right_product(self_low, out_whole))
@@ -334,7 +771,6 @@
     table_full = jnp.einsum(
         "hij,ijb->bh", jnp.sum(bias_part, axis=0), bucket_hot, precision=PRECISE
     )
-    bucket_table_grad = lax.psum(table_full, ("dp", "fsdp"))
     query_full = left_product(first_norm, query_low)
     key_full = left_product(first_norm, key_low)
     value_full = left_product(first_norm, value_low)
@@ -348,14 +784,14 @@
     hidden_in_grad = mid_grad + state_back
     sequence_sums = jnp.sum(hidden_in_grad.reshape(seq_count, length, width), axis=1)
     language_full = left_product(language_hot, sequence_sums)
-    sgain_part, language_part, query_sum, key_sum, value_sum, out_part = (
-        lax.psum_scatter(self_gain_full, ("dp", "fsdp"), scatter_dimension=0, tiled=True),
-        lax.psum_scatter(language_full, ("dp", "fsdp"), scatter_dimension=1, tiled=True),
-        lax.psum_scatter(query_full, ("dp", "fsdp"), scatter_dimension=0, tiled=True),
-        lax.psum_scatter(key_full, ("dp", "fsdp"), scatter_dimension=0, tiled=True),
-        lax.psum_scatter(value_full, ("dp", "fsdp"), scatter_dimension=0, tiled=True),
-        lax.psum_scatter(out_full, ("dp", "fsdp"), scatter_dimension=0, tiled=True),
-    )
+    (
+        language_part, bucket_table_grad, sgain_part, cgain_part, feed_gain_part, whole_parts, inner_part, outer_part,
+    ) = reduce_grads(
+        sizes, language_full, table_full, (self_gain_full, cross_gain_full, feed_gain_full),
+        (query_full, key_full, value_full, out_full, cquery_full, ckey_full, cvalue_full, cout_full),
+        inner_full, outer_full,
+    )
+    query_sum, key_sum, value_sum, out_part, cquery_part_sum, ckey_part_sum, cvalue_part_sum, cout_part = whole_parts
     return (
         hidden_out,
         hidden_in_grad,
@@ -379,6 +815,7 @@
 
 
 def solution(mesh):
+    sizes = (mesh.shape["dp"] // 2, mesh.shape["fsdp"] // 2)
     in_specs = (
         P(("dp", "fsdp"), None),
         P(("dp", "fsdp"), None),
@@ -422,4 +859,4 @@
         P(("dp", "fsdp"), None),
         P(("dp", "fsdp"), None),
     )
-    return jax.shard_map(local, mesh=mesh, in_specs=in_specs, out_specs=out_specs, check_vma=False)
+    return jax.shard_map(functools.partial(local, sizes), mesh=mesh, in_specs=in_specs, out_specs=out_specs, check_vma=False)

time: 1740 us -> 544 us (0.31)
  waiting for transfers between devices: 1250 us -> 0 us
  Pallas kernels: 0 us -> 235 us
  blocking collectives: 150 us -> 0 us
  matrix products: 190 us -> 159 us
  local copies, waits for them, and re-layouts: 96.8 us -> 117 us
    reduce_scatter x8 -> x0, waiting for transfers between devices: 771 us -> none  [the longest x1 142 us: local(): lax.psum_scatter(inner_full, ('dp', 'fsdp'), scatter_dimension=0, tiled=T...]
    all_gather x10 -> x0, waiting for transfers between devices: 373 us -> none  [the longest x1 62.2 us: local(): lax.all_gather(outer_weight, ('dp', 'fsdp'), axis=0, tiled=True)]
    pallas_call x0 -> x2, Pallas kernels: none -> 235 us  [the longest x1 125 us: gather_weights(): pl.pallas_call(functools.partial(gather_kernel, sizes), out_shape=[jax.Sh...]
    unnamed x22 -> x0, waiting for transfers between devices: 110 us -> none
    unnamed x2 -> x0, blocking collectives: 83.2 us -> none
    all_gather x1 -> x0, blocking collectives: 66.5 us -> none  [local(): lax.all_gather(language_table, ('dp', 'fsdp'), axis=1, tiled=True)]
    reshape x0 -> x7, local copies, waits for them, and re-layouts: none -> 20 us  [the longest x2 9.99 us: local(): to_low(matmul(encoder_flat, ckey_whole)).reshape(enc_count, enc_length, -1)]
    unnamed x135 -> x186, local copies, waits for them, and re-layouts: 37.7 us -> 33.2 us
  transfers between devices with their start and end apart: 20 -> 0, of which waited for: 16 -> 0; matrix products, arithmetic and copies ran while one was open for 15% -> 0% of each run, Pallas kernels for 0% -> 0%
where the time goes in v1:
time: 544 us; the launch traced here: 535 us
  Pallas kernels  235 us (43%)
  matrix products  159 us (29%)
  local copies, waits for them, and re-layouts  117 us (22%)
  other arithmetic  22 us (4%)
    pallas_call x1, Pallas kernels, gather_weights(): pl.pallas_call(functools.partial(gather_kernel, sizes), out_shape=[jax.Sh...  125 us
    pallas_call x1, Pallas kernels, reduce_grads(): pl.pallas_call(functools.partial(reduce_kernel, sizes, tuple((len(s) for...  110 us
    unnamed x186, local copies, waits for them, and re-layouts  33.2 us
    dot_general x10, matrix products, matmul(): return jnp.dot(left, right, preferred_element_type=jnp.float32)  31.1 us
    dot_general x11, matrix products, left_product(): lax.dot_general(left, right, (((0,), (0,)), ((), ())), preferred_element_...  26.1 us
    convert_element_type x16, local copies, waits for them, and re-layouts, to_low(): return value.astype(jnp.bfloat16)  23.9 us
    dot_general x10, matrix products, right_product(): lax.dot_general(left, right, (((1,), (1,)), ((), ())), preferred_element_...  22.6 us
    dot_general x2, matrix products, attend_backward(): jnp.einsum('sqhe,skhe->shqk', grad_heads, split_heads(value_rows), prefer...  12 us

profile of v1, /device:TPU:0, one launch (start us, length us, event | category | flops | bytes accessed | tf_op | source)
XLA Modules:
  0.0 535.2 jit_solution(1059934812310123160)
XLA Ops:
  0.7 4.8 select_bitcast_fusion
  5.5 4.9 copy.126
  11.6 125.4 %shard_map.340 = (bf16[2,2,4,2,16,128]{5,4,3,2,1,0:T(8,128)(2,1)}, bf16[2,2,4,2,24,768]{5,4,3,2,1,0:T(8,128)(2,1)}, bf16[2,2,4,2,24,768]{5,4,3,2,1,0:T(8,128)(2,...) custom-call(bf16[16,128]{1,0:T(8,128)(2,1)} %copy-done.59, ...), custom_call_target="tpu_custom_call" | custom-call | tf_op jit(solution)/shard_map/pallas_call | solution.py:277
  141.2 2.6 convolution_convert_fusion.22
  144.9 2.7 reshape.553
  147.6 3.3 add_reduce_fusion
  153.6 3.0 fusion.15
  157.9 2.7 fusion.34
  163.4 2.6 fusion.25
  166.0 3.9 reshape.560
  169.9 6.1 %copy.131 = bf16[2,512,768]{2,0,1:T(2,128)(2,1)} copy(bf16[2,512,768]{1,0,2:T(2,128)(2,1)} %reshape.560) | data formatting | bytes 3145728 | tf_op jit(solution)/shard_map/reshape | solution.py:654
  176.0 4.8 convolution_convert_fusion.5
  180.8 5.0 copy.132
  185.8 3.9 fusion.26
  189.7 3.9 reshape.565
  193.6 6.1 %copy.135 = bf16[2,512,768]{2,0,1:T(2,128)(2,1)} copy(bf16[2,512,768]{1,0,2:T(2,128)(2,1)} %reshape.565) | data formatting | bytes 3145728 | tf_op jit(solution)/shard_map/reshape | solution.py:653
  199.7 4.8 convolution_convert_fusion.4
  204.5 4.9 copy.136
  209.5 3.0 convolution_convert_fusion.19
  214.8 2.9 reshape.563
  217.7 3.6 fusion.79
  221.3 3.1 exponential_reduce_fusion
  226.0 3.2 fusion.30
  232.5 5.4 %fusion.75 = f32[512,3072]{1,0:T(8,128)S(1)} fusion(bf16[768,3072]{1,0:T(8,128)(2,1)} %bitcast.251, f32[512,768]{1,0:T(8,128)} %get-tuple-element.298, f32[768]{0:T(1024)S(1)} %reshape.593, f32[512]{0:T(512)S(1)} %fusion.65), kind=kOutput, calls=%fused_computation.153 | convolution fusion | flops 2417098752 | bytes 12588032 | tf_op jit(solution)/shard_map/dot_general | solution.py:29
  238.0 9.3 %add_convert_fusion = bf16[512,768]{1,0:T(8,128)(2,1)} fusion(f32[512,768]{1,0:T(8,128)S(1)} %copy-done.16, bf16[3072,768]{1,0:T(8,128)(2,1)} %bitcast.297, f32[512,3072]{1,0:T(8,128)S(1)} %fusion.75), kind=kOutput, calls=%fused_computation.61 | convolution fusion | flops 2430861312 | bytes 13369344 | tf_op jit(solution)/shard_map/dot_general | solution.py:29
  247.3 6.1 %fusion.9 = bf16[512,3072]{1,0:T(8,128)(2,1)S(1)} fusion(f32[512,3072]{1,0:T(8,128)S(1)} %fusion.75, bf16[3072,768]{1,0:T(8,128)(2,1)S(1)} %bitcast.300, bf16[512,768]{1,0:T(8,128)(2,1)S(1)} %copy-done.56), kind=kOutput, calls=%fused_computation.16 | convolution fusion | flops 2447376384 | bytes 14942208 | tf_op jit(solution)/shard_map/dot_general | solution.py:39
  253.5 2.8 multiply_reduce_fusion.2
  262.0 2.9 reshape.571
  264.9 7.7 %multiply_reduce_fusion = (f32[2,12,256]{2,1,0:T(8,128)S(1)}, f32[2,12,256,512]{3,2,1,0:T(8,128)S(1)}) fusion(f32[2,12,256,512]{3,2,1,0:T(8,128)} %copy-done.1, f32[2,12,256]{2,1,0:T(8,128)S(1)} %log_add_fusion, bf16[2,512,12,64]{1,3,2,0:T(8,128)(2,1)} %bitcast.240, bf16[2,256,12,64]{1,0,3,2:T(2,128)(2,1)} %reshape.571), kind=kOutput, calls=%fused_computation.1 | convolution fusion | flops 412084224 | bytes 27574272 | tf_op jit(solution)/shard_map/while/body/eval_jaxpr/sqhe,skhe->shqk/dot_general | solution.py:77
  272.6 6.9 %multiply_convert_fusion = bf16[2,12,256,512]{3,2,1,0:T(8,128)(2,1)S(1)} fusion(f32[2,12,256,512]{3,2,1,0:T(8,128)S(1)} %get-tuple-element.301, f32[2,12,256,512]{3,2,1,0:T(8,128)} %copy-done.1, f32[2,12,256]{2,1,0:T(8,128)S(1)} %get-tuple-element.300, f32[2,12,256]{2,1,0:T(8,128)S(1)} %log_add_fusion), kind=kLoop, calls=%fused_computation | loop fusion | flops 12582912 | bytes 31506432 | tf_op jit(solution)/shard_map/while/body/eval_jaxpr/convert_element_type | solution.py:21
  290.5 2.9 reshape.572
  293.4 3.3 fusion.37
  298.6 4.4 multiply_reduce_fusion.1
  303.0 4.6 convert_reduce_fusion
  318.6 2.9 fusion.45
  321.4 6.0 %copy.156 = f32[2,512,768]{2,0,1:T(2,128)} copy(f32[2,512,768]{1,2,0:T(8,128)} %bitcast.242) | data formatting | bytes 6291456 | tf_op jit(solution)/shard_map/reshape | solution.py:721
  327.4 7.8 %convolution_convert_fusion.3 = bf16[2,512,768]{2,0,1:T(2,128)(2,1)S(1)} fusion(f32[2,512,768]{2,0,1:T(2,128)} %copy.156, s32[2]{0:T(128)S(1)} %copy-done.69), kind=kOutput, calls=%fused_computation.42 | convolution fusion | flops 19660804 | bytes 4718600 | tf_op jit(solution)/shard_map/se,smc->emc/dot_general | solution.py:718
  337.0 3.1 fusion.82
  340.1 7.6 %fusion.16 = f32[2,12,64,512]{3,2,1,0:T(8,128)} fusion(f32[2,12,256,512]{3,2,1,0:T(8,128)} %copy-done.1, f32[2,12,256]{2,1,0:T(8,128)S(1)} %log_add_fusion, bf16[2,256,12,64]{1,0,3,2:T(2,128)(2,1)S(1)} %copy-done.29), kind=kOutput, calls=%fused_computation.47 | convolution fusion | flops 408944640 | bytes 16539648 | tf_op jit(solution)/shard_map/while/body/eval_jaxpr/shqk,sqhe->skhe/dot_general | solution.py:74
  347.7 5.8 %copy.159 = f32[2,512,768]{2,0,1:T(2,128)} copy(f32[2,512,768]{1,2,0:T(8,128)} %bitcast.243) | data formatting | bytes 6291456 | tf_op jit(solution)/shard_map/reshape | solution.py:729
  353.5 8.3 %convolution_convert_fusion.2 = bf16[2,512,768]{2,0,1:T(2,128)(2,1)S(1)} fusion(f32[2,512,768]{2,0,1:T(2,128)} %copy.159, s32[2]{0:T(128)S(1)} %copy-done.69), kind=kOutput, calls=%fused_computation.41 | convolution fusion | flops 19660804 | bytes 4718600 | tf_op jit(solution)/shard_map/se,smc->emc/dot_general | solution.py:726
  363.7 3.1 convolution_add_fusion
  376.3 2.5 bitcast_convert_fusion.1
  383.1 4.6 convolution_convert_fusion.1
  387.8 5.0 convolution_convert_fusion
  393.1 5.4 %copy.165 = f32[12,256,256]{2,0,1:T(8,128)} copy(f32[12,256,256]{1,2,0:T(8,128)} %get-tuple-element.281) | data formatting | bytes 6291456 | tf_op jit(solution)/shard_map/while/body/eval_jaxpr/reduce_sum | solution.py:93
  398.5 6.1 %fusion.38 = f32[32,12]{1,0:T(8,128)S(1)} fusion(f32[12,256,256]{2,0,1:T(8,128)} %copy.165, s32[256,256]{1,0:T(8,128)S(1)} %copy-done.48), kind=kOutput, calls=%fused_computation.97 | convolution fusion | flops 304087040 | bytes 3409408 | tf_op jit(solution)/shard_map/hij,ijb->bh/dot_general | solution.py:771
  406.0 110.0 %shard_map.341 = (f32[24,768]{1,0:T(8,128)}, f32[24,768]{1,0:T(8,128)}, f32[24,768]{1,0:T(8,128)}, f32[24,768]{1,0:T(8,128)}, f32[24,768]{1,0:T(8,128)}, /*index...) custom-call(bf16[2,2,4,2,24,768]{5,4,3,2,1,0:T(8,128)(2,1)} %bitcast, ...), custom_call_target="tpu_custom_call" | custom-call | tf_op jit(solution)/shard_map/pallas_call | solution.py:539
  (265 shorter events, 87.4 us)
Async XLA Ops:
  0.7 162.5 %copy-start = (bf16[2,512,768]{2,1,0:T(8,128)(2,1)S(1)}, bf16[2,512,768]{2,1,0:T(8,128)(2,1)}, u32[]{:S(2)}) copy-start(bf16[2,512,768]{2,1,0:T(8,128)(2,1)} %param.33) | copy-start | bytes 4718596
  5.5 5.0 copy-start.60
  5.5 5.0 copy-start.61
  5.5 5.1 copy-start.62
  5.5 5.3 copy-start.63
  5.5 132.7 %copy-start.70 = (s32[2]{0:T(128)S(1)}, s32[2]{0:T(128)}, u32[]{:S(2)}) copy-start(s32[2]{0:T(128)} %param.34) | copy-start | bytes 28
  10.5 128.0 %copy-start.6 = (bf16[512,768]{1,0:T(8,128)(2,1)S(1)}, bf16[512,768]{1,0:T(8,128)(2,1)}, u32[]{:S(2)}) copy-start(bf16[512,768]{1,0:T(8,128)(2,1)} %param.31) | copy-start | bytes 2359300
  141.2 6.4 %copy-start.27 = (bf16[2,256,12,64]{1,0,3,2:T(2,128)(2,1)}, bf16[2,256,12,64]{1,0,3,2:T(2,128)(2,1)S(1)}, u32[]{:S(2)}) copy-start(bf16[2,256,12,64]{1,0,3,2:T(2,128)(2,1)S(1)} %reshape.555) | copy-start | bytes 2359300
  147.6 3.3 copy-start.25
  147.6 3.3 copy-start.2
  150.9 2.7 copy-start.4
  153.6 3.0 copy-start.42
  153.6 3.0 copy-start.50
  157.9 2.8 copy-start.20
  169.9 6.1 %copy-start.69 = (s32[2]{0:T(128)S(1)}, s32[2]{0:T(128)}, u32[]{:S(2)}) copy-start(s32[2]{0:T(128)} %param.35) | copy-start | bytes 28
  221.2 4.7 copy-start.1
  221.2 4.7 copy-start.18
  232.5 5.4 %copy-start.16 = (f32[512,768]{1,0:T(8,128)S(1)}, f32[512,768]{1,0:T(8,128)}, u32[]{:S(2)}) copy-start(f32[512,768]{1,0:T(8,128)} %get-tuple-element.298) | copy-start | bytes 4718596
  232.5 14.8 %slice-start.8 = ((s8[4718592]{0:T(1024)(128)(4,1)}), s8[4194304]{0:T(1024)(128)(4,1)S(1)}, s32[]{:S(2)}) async-start(s8[4718592]{0:T(1024)(128)(4,1)} %bitcast.298), calls=%async_computation.8 | async-start | bytes 8388608
  238.0 9.3 %copy-start.32 = (f32[512,3072]{1,0:T(8,128)}, f32[512,3072]{1,0:T(8,128)S(1)}, u32[]{:S(2)}) copy-start(f32[512,3072]{1,0:T(8,128)S(1)} %fusion.75) | copy-start | bytes 18874372
  238.0 9.3 %copy-start.56 = (bf16[512,768]{1,0:T(8,128)(2,1)S(1)}, bf16[512,768]{1,0:T(8,128)(2,1)}, u32[]{:S(2)}) copy-start(bf16[512,768]{1,0:T(8,128)(2,1)} %param.32) | copy-start | bytes 2359300
  238.0 9.3 %slice-start.9 = ((s8[4718592]{0:T(1024)(128)(4,1)}), s8[524288]{0:T(1024)(128)(4,1)S(1)}, s32[]{:S(2)}) async-start(s8[4718592]{0:T(1024)(128)(4,1)} %bitcast.298), calls=%async_computation.9 | async-start | bytes 1048576
  238.0 15.5 %slice-start.6 = ((s8[4718592]{0:T(1024)(128)(4,1)}), s8[4194304]{0:T(1024)(128)(4,1)S(1)}, s32[]{:S(2)}) async-start(s8[4718592]{0:T(1024)(128)(4,1)} %bitcast.252), calls=%async_computation.6 | async-start | bytes 8388608
  247.3 6.2 %slice-start.7 = ((s8[4718592]{0:T(1024)(128)(4,1)}), s8[524288]{0:T(1024)(128)(4,1)S(1)}, s32[]{:S(2)}) async-start(s8[4718592]{0:T(1024)(128)(4,1)} %bitcast.252), calls=%async_computation.7 | async-start | bytes 1048576
  253.5 2.9 copy-start.72
  272.6 6.9 %copy-start.15 = (bf16[2,512,768]{1,2,0:T(8,128)(2,1)S(1)}, bf16[2,512,768]{1,2,0:T(8,128)(2,1)}, u32[]{:S(2)}) copy-start(bf16[2,512,768]{1,2,0:T(8,128)(2,1)} %copy.136) | copy-start | bytes 4718596
  279.5 2.7 copy-start.5
  293.4 4.3 copy-start.21
  293.4 4.3 copy-start.22
  297.7 17.4 %copy-start.36 = (bf16[96,8,2,256]{3,1,2,0:T(8,128)(2,1)}, bf16[96,8,2,256]{3,1,2,0:T(8,128)(2,1)S(1)}, u32[]{:S(2)}) copy-start(bf16[96,8,2,256]{3,1,2,0:T(8,128)(2,1)S(1)} %copy.187) | copy-start | bytes 2359300
  297.7 5.3 slice-start
  298.6 4.4 slice-start.1
  303.0 4.7 copy-start.28
  314.2 4.3 slice-start.2
  315.1 3.4 slice-start.3
  337.0 3.1 copy-start.29
  353.5 8.5 %copy-start.41 = (bf16[2,2,4,2,24,768]{5,4,3,2,1,0:T(8,128)(2,1)S(1)}, bf16[2,2,4,2,24,768]{5,4,3,2,1,0:T(8,128)(2,1)}, u32[]{:S(2)}) copy-start(bf16[2,2,4,2,24,768]{5,4,3,2,1,0:T(8,128)(2,1)} %get-tuple-element.204) | copy-start | bytes 3538948
  363.7 3.1 copy-start.51
  363.7 3.1 copy-start.53
  378.8 2.5 copy-start.11
  378.8 2.5 copy-start.24
  378.8 4.3 copy-start.73
  381.3 6.4 %slice-start.4 = ((s8[6291456]{0:T(1024)(128)(4,1)}), s8[4194304]{0:T(1024)(128)(4,1)S(1)}, s32[]{:S(2)}) async-start(s8[6291456]{0:T(1024)(128)(4,1)} %bitcast.248), calls=%async_computation.4 | async-start | bytes 8388608
  383.1 4.6 slice-start.5
  383.1 4.6 copy-start.57
  387.8 5.0 copy-start.71
  393.1 5.4 %copy-start.48 = (s32[256,256]{1,0:T(8,128)S(1)}, s32[256,256]{1,0:T(8,128)}, u32[]{:S(2)}) copy-start(s32[256,256]{1,0:T(8,128)} %param.36) | copy-start | bytes 786436
  516.1 18.2 %copy-start.58 = (f32[4,24,768]{2,1,0:T(8,128)S(1)}, f32[4,24,768]{2,1,0:T(8,128)}, u32[]{:S(2)}) copy-start(f32[4,24,768]{2,1,0:T(8,128)} %get-tuple-element.220) | copy-start | bytes 884740
  (36 other events, 55.6 us)
